TPU v7x, 512 devices: a whole 4x4x16 slice. The times are simulated.
512 devices in a mesh: vocab: 32 (over x, y, core), dp: 16 (over z).
Axes of the slice: x: 4, y: 4, z: 16, core: 2. Of those that a mesh axis runs over, the one named last changes fastest.
Arguments:
- hidden: bfloat16 [2048, 2048], P('dp', 'vocab')
- head_weight: bfloat16 [2048, 65536], P('dp', 'vocab')
- teacher_logits: bfloat16 [2048, 65536], P('dp', 'vocab')
- target_ids: int32 [2048], P('dp'), may hold values from 0 to 65535
- segment_ids: int32 [16, 128], P('dp'), may hold values from 0 to 15, never falling along the last dimension, each value on 1 to 16 neighbouring positions
- pair_order: int32 [16, 16], P('dp'), may hold values from 0 to 15, each once within a row
Outputs:
- hidden_grad: bfloat16 [2048, 2048], P('dp', 'vocab')
- head_grad: float32 [2048, 65536], P('dp', 'vocab')
- loss: float32 [], replicated
Inputs may be any that keep to these rules, and one draw needn't show every extreme that they name: `segment_ids`: in each group the row's sequence number never falls along the rows, and every sequence has 1 to 16 rows. `pair_order`: each group's row is a permutation of its 16 sequences; pair p is entry 2p (chosen) and entry 2p + 1 (rejected).
All inputs are finite; a program needn't handle non-finite values.
Results may differ from a plain program's by a relative error of at most 0.018.
Values may be sent and summed in bfloat16 or wider, within the bound.
No kernel may reach another device: no remote copies, remote signals or barrier semaphores. Data moves between devices by JAX's collectives and lax.ppermute only.
A program may use at most 64 MiB of HBM per device.

v0:
```python
import jax
import jax.numpy as jnp
from jax import lax
from jax.sharding import PartitionSpec as P

dpo_beta = 0.1
dpo_gamma = 4.0


def pair_weights(log_ratio, segments, ordering):
    seq_count = ordering.shape[0]
    labels = lax.broadcasted_iota(jnp.int32, (1, seq_count), 1)
    seq_hot = (segments[:, None] == labels).astype(jnp.float32)
    seq_ratio = jnp.sum(seq_hot * log_ratio[:, None], axis=0)
    chosen = ordering[0::2]
    rejected = ordering[1::2]
    chosen_hot = (chosen[:, None] == labels).astype(jnp.float32)
    rejected_hot = (rejected[:, None] == labels).astype(jnp.float32)
    margin = dpo_beta * (
        jnp.sum(chosen_hot * seq_ratio[None, :], axis=1)
        - jnp.sum(rejected_hot * seq_ratio[None, :], axis=1)
    )
    strength = dpo_gamma * dpo_beta * jax.nn.sigmoid(-margin)
    coeffs = jnp.sum((rejected_hot - chosen_hot) * strength[:, None], axis=0)
    row_weight = jnp.sum(seq_hot * coeffs[None, :], axis=1)
    return (row_weight, jnp.sum(jax.nn.softplus(-margin)))


def on_device(hidden, head_weight, teacher_logits, target_ids, segment_ids, pair_order):
    rows_full = lax.all_gather(hidden, "vocab", axis=1, tiled=True)
    weight_full = lax.all_gather(head_weight, "dp", axis=0, tiled=True)
    student = jnp.dot(rows_full, weight_full, preferred_element_type=jnp.float32)
    teacher = teacher_logits.astype(jnp.float32)
    shard_width = student.shape[1]
    offset = lax.axis_index("vocab") * shard_width
    column = lax.broadcasted_iota(jnp.int32, student.shape, 1) + offset
    is_target = column == target_ids[:, None]
    local_target = jnp.sum(jnp.where(is_target, student, 0.0), axis=1)
    local_tgt_teach = jnp.sum(jnp.where(is_target, teacher, 0.0), axis=1)
    local_max = jnp.max(student, axis=1)
    local_tmax = jnp.max(teacher, axis=1)
    max_student, max_teacher = lax.pmax((local_max, local_tmax), "vocab")
    exp_student = jnp.exp(student - max_student[:, None])
    exp_teacher = jnp.exp(teacher - max_teacher[:, None])
    sum_student, sum_teacher, cross, target_student, target_teacher = lax.psum(
        (
            jnp.sum(exp_student, axis=1),
            jnp.sum(exp_teacher, axis=1),
            jnp.sum(exp_teacher * (teacher - student), axis=1),
            local_target,
            local_tgt_teach,
        ),
        "vocab",
    )
    lse_student = max_student + jnp.log(sum_student)
    lse_teacher = max_teacher + jnp.log(sum_teacher)
    kl_rows = cross / sum_teacher - lse_teacher + lse_student
    log_ratio = target_student - lse_student - (target_teacher - lse_teacher)
    row_weight, dpo_sum = pair_weights(log_ratio, segment_ids[0], pair_order[0])
    group_objective = jnp.sum(kl_rows) + dpo_gamma * dpo_sum
    summed_objective = lax.psum(group_objective, "dp")
    loss_value = summed_objective / (rows_full.shape[0] * lax.axis_size("dp"))
    prob_student = exp_student / sum_student[:, None]
    prob_teacher = exp_teacher / sum_teacher[:, None]
    logit_grad = (
        prob_student
        - prob_teacher
        + row_weight[:, None] * (is_target.astype(jnp.float32) - prob_student)
    ).astype(jnp.bfloat16)
    hidden_term = lax.dot_general(
        logit_grad, weight_full, (((1,), (1,)), ((), ())), preferred_element_type=jnp.float32
    )
    hidden_grad = lax.psum_scatter(
        hidden_term.astype(jnp.bfloat16), "vocab", scatter_dimension=1, tiled=True
    )
    grad_cols = lax.all_to_all(rows_full, "dp", split_axis=1, concat_axis=0, tiled=True)
    head_grad = lax.dot_general(
        grad_cols,
        lax.all_gather(logit_grad, "dp", axis=0, tiled=True),
        (((0,), (0,)), ((), ())),
        preferred_element_type=jnp.float32,
    )
    return (hidden_grad, head_grad, loss_value)


def solution(mesh):
    return jax.shard_map(
        on_device,
        mesh=mesh,
        in_specs=(
            P("dp", "vocab"),
            P("dp", "vocab"),
            P("dp", "vocab"),
            P("dp"),
            P("dp", None),
            P("dp", None),
        ),
        out_specs=(P("dp", "vocab"), P("dp", "vocab"), P()),
        check_vma=False,
    )
```

profile of v0, /device:TPU:2, one launch (start us, length us, event | category | flops | bytes accessed | tf_op | source)
XLA Modules:
  0.0 486.9 jit_solution(1537256044486397161)
XLA Ops:
  7.2 0.0 all-gather.3.cloned.1.call-start
  7.2 0.7 all-gather.3.cloned.1.call-update
  7.9 0.0 copy-start
  7.9 0.0 all-gather.5.cloned.1.call-start
  8.0 0.8 slice.7
  8.8 0.7 slice.6
  9.5 1.2 reduce_max.24
  10.7 29.9 %all_gather.9 = bf16[128,2048]{0,1:T(8,128)(2,1)} all-gather(bf16[128,64]{0,1:T(8,128)(2,1)} %param.6), channel_id=1, replica_groups=mesh['vocab'=32,'dp'=16] {'vocab'}, dimensions={1}, use_global_device_ids=true | all-gather | bytes 540672 | tf_op jit(solution)/shard_map/all_gather | solution.py:30
  40.6 79.9 %all-gather.3.cloned.1.call-done = bf16[2048,2048]{1,0:T(8,128)(2,1)} async-done(((bf16[128,2048]{1,0:T(8,128)(2,1)}), bf16[2048,2048]{1,0:T(8,128)(2,1)}) %all-gather.3.cloned.1.call-update) | async-done | bytes 8388624 | tf_op jit(solution)/shard_map/all_gather | solution.py:31
  120.5 4.9 %fusion.14 = (f32[128]{0:T(128)S(1)}, f32[128,2048]{1,0:T(8,128)S(1)}) fusion(bf16[128,2048]{0,1:T(8,128)(2,1)} %all_gather.9, bf16[2048,2048]{1,0:T(8,128)(2,1)} %all-gather.3.cloned.1.call-done), kind=kOutput, calls=%fused_computation.38 | convolution fusion | flops 1074003840 | bytes 9961984 | tf_op jit(solution)/shard_map/dot_general | solution.py:32
  125.4 56.2 %all-reduce.1 = (f32[128]{0:T(128)S(1)}, f32[128]{0:T(128)S(1)}) all-reduce(bf16[128]{0:T(256)(128)(2,1)S(1)} %reduce_max.24, f32[128]{0:T(128)S(1)} %get-tuple-element.33), channel_id=1, replica_groups=mesh['vocab'=32,'dp'=16] {'vocab'}, use_global_device_ids=true, to_apply=%region_5.6 | all-reduce | flops 256 | bytes 1792 | tf_op jit(solution)/shard_map/pmax | solution.py:42
  181.6 0.8 fusion.6
  182.4 56.8 %all-reduce = (f32[128]{0:T(128)S(1)}, f32[128]{0:T(128)S(1)}, f32[128]{0:T(128)S(1)}, f32[128]{0:T(128)S(1)}, f32[128]{0:T(128)S(1)}) all-reduce(f32[128]{0:T(128)S(1)} %get-tuple-element.18, f32[128]{0:T(128)S(1)} %get-tuple-element.16, f32[128]{0:T(128)S(1)} %get-tuple-element.19, ...), channel_id=1, replica_groups=mesh['vocab'=32,'dp'=16] {'vocab'}, use_global_device_ids=true, to_apply=%region_11.12 | all-reduce | flops 640 | bytes 5120 | tf_op jit(solution)/shard_map/psum | solution.py:45
  239.2 0.6 add_reduce_fusion
  239.9 0.1 select_reduce_fusion.1
  240.0 0.2 select_reduce_fusion.2
  240.2 0.6 fusion.13
  240.8 0.1 multiply_reduce_fusion
  240.9 0.1 select_reduce_fusion
  241.0 1.4 fusion.11
  242.4 0.0 all-gather.5.cloned.1.call-update
  242.4 8.9 %all-to-all-start = ((bf16[128,16,128]{0,2,1:T(8,128)(2,1)}), bf16[128,16,128]{0,2,1:T(8,128)(2,1)S(1)}, u32[]{:S(2)}, u32[]{:S(2)}) async-start(bf16[128,16,128]{0,2,1:T(8,128)(2,1)} %bitcast.2), calls=%async_computation.1 | async-start | bytes 1048576 | tf_op jit(solution)/shard_map/all_to_all | solution.py:76
  251.3 0.0 reduce-scatter.2.cloned.1.call-start
  251.4 6.7 %convolution_convert_fusion = bf16[128,2048]{0,1:T(8,128)(2,1)} fusion(bf16[128,2048]{1,0:T(8,128)(2,1)} %fusion.11, bf16[2048,2048]{1,0:T(8,128)(2,1)} %all-gather.3.cloned.1.call-done), kind=kOutput, calls=%fused_computation.1 | convolution fusion | flops 1074003968 | bytes 9437184 | tf_op jit(solution)/shard_map/dot_general | solution.py:70
  258.1 0.0 reduce-scatter.2.cloned.1.call-update
  259.3 21.5 %all-to-all-done = bf16[128,16,128]{0,2,1:T(8,128)(2,1)S(1)} async-done(((bf16[128,16,128]{0,2,1:T(8,128)(2,1)}), bf16[128,16,128]{0,2,1:T(8,128)(2,1)S(1)}, u32[]{:S(2)}, u32[]{:S(2)}) %all-to-all-start) | async-done | bytes 524320 | tf_op jit(solution)/shard_map/all_to_all | solution.py:76
  280.9 0.3 copy.13
  281.1 32.6 %psum.47 = f32[]{:T(128)} all-reduce(f32[]{:T(128)S(6)} %add.55), channel_id=1, replica_groups=mesh['vocab'=32,'dp'=16] {'dp'}, use_global_device_ids=true, to_apply=%region_22.23 | all-reduce | flops 1 | bytes 8 | tf_op jit(solution)/shard_map/psum | solution.py:61
  314.4 48.8 %all-gather.5.cloned.1.call-done = bf16[2048,2048]{1,0:T(8,128)(2,1)} async-done(((bf16[128,2048]{1,0:T(8,128)(2,1)}), bf16[2048,2048]{1,0:T(8,128)(2,1)}) %all-gather.5.cloned.1.call-update) | async-done | bytes 8388624 | tf_op jit(solution)/shard_map/all_gather | solution.py:79
  363.2 5.8 %convolution_bitcast_fusion = f32[128,2048]{0,1:T(8,128)S(1)} fusion(bf16[2048,2048]{1,0:T(8,128)(2,1)} %all-gather.5.cloned.1.call-done, bf16[2048,128]{1,0:T(8,128)(2,1)S(1)} %bitcast.14), kind=kOutput, calls=%fused_computation | convolution fusion | flops 1073741824 | bytes 9961472 | tf_op jit(solution)/shard_map/dot_general | solution.py:77
  369.0 1.3 copy.14
  370.3 109.0 %reduce-scatter.2.cloned.1.call-done = bf16[128,64]{0,1:T(8,128)(2,1)} async-done(((bf16[128,2048]{0,1:T(8,128)(2,1)}), bf16[128,64]{0,1:T(8,128)(2,1)}) %reduce-scatter.2.cloned.1.call-update) | async-done | bytes 16400 | tf_op jit(solution)/shard_map/reduce_scatter | solution.py:73
  (6 shorter events, 0.0 us)
Async XLA Ops:
  7.2 113.3 %all-gather.3.cloned.1.call-start = ((), (), s32[]{:S(2)}) async-start(), calls=%async_computation.2 | async-start | bytes 8912896 | tf_op jit(solution)/shard_map/all_gather | solution.py:31
  7.9 173.7 %copy-start = (bf16[128,2048]{1,0:T(8,128)(2,1)S(1)}, bf16[128,2048]{1,0:T(8,128)(2,1)}, u32[]{:S(2)}) copy-start(bf16[128,2048]{1,0:T(8,128)(2,1)} %param.8) | copy-start | bytes 1572868
  7.9 173.7 %copy-start.1 = (s32[128]{0:T(128)S(1)}, s32[128]{0:T(128)}, u32[]{:S(2)}) copy-start(s32[128]{0:T(128)} %param.9) | copy-start | bytes 1540
  7.9 355.3 %all-gather.5.cloned.1.call-start = ((), (), s32[]{:S(2)}) async-start(), calls=%async_computation.4 | async-start | bytes 8912896 | tf_op jit(solution)/shard_map/all_gather | solution.py:79
  40.6 199.2 %copy-start.2 = (s32[1,128]{1,0:T(1,128)S(1)}, s32[1,128]{1,0:T(1,128)}, u32[]{:S(2)}) copy-start(s32[1,128]{1,0:T(1,128)} %param.10) | copy-start | bytes 1540
  242.4 38.4 %all-to-all-start = ((bf16[128,16,128]{0,2,1:T(8,128)(2,1)}), bf16[128,16,128]{0,2,1:T(8,128)(2,1)S(1)}, u32[]{:S(2)}, u32[]{:S(2)}) async-start(bf16[128,16,128]{0,2,1:T(8,128)(2,1)} %bitcast.2), calls=%async_computation.1 | async-start | bytes 1048576 | tf_op jit(solution)/shard_map/all_to_all | solution.py:76
  251.3 227.9 %reduce-scatter.2.cloned.1.call-start = ((), (), s32[]{:S(2)}) async-start(), calls=%async_computation.3 | async-start | bytes 540672 | tf_op jit(solution)/shard_map/reduce_scatter | solution.py:73
Sparse Core Ops, SparseCore 0:
  10.1 110.3 all-gather.2
  242.6 120.6 all-gather.4
  368.1 111.0 reduce-scatter.1
where the time goes:
time: 487 us
  waiting for transfers between devices  260 us (53%)
  blocking collectives  175 us (36%)
  matrix products  17.4 us (4%)
  between operations  16.8 us (3%)
  starting transfers between devices  9 us (2%)
  other arithmetic  5.2 us (1%)
    reduce_scatter x1, waiting for transfers between devices, on_device(): lax.psum_scatter(hidden_term.astype(jnp.bfloat16), 'vocab', scatter_dimen...  109 us
    all_gather x1, waiting for transfers between devices, on_device(): weight_full = lax.all_gather(head_weight, 'dp', axis=0, tiled=True)  79.9 us
    psum x1, blocking collectives, on_device(): lax.psum((jnp.sum(exp_student, axis=1), jnp.sum(exp_teacher, axis=1), jnp...  56.8 us
    pmax x1, blocking collectives, on_device(): max_student, max_teacher = lax.pmax((local_max, local_tmax), 'vocab')  56.2 us
    all_gather x1, waiting for transfers between devices, on_device(): lax.all_gather(logit_grad, 'dp', axis=0, tiled=True)  48.8 us
    psum x1, blocking collectives, on_device(): summed_objective = lax.psum(group_objective, 'dp')  32.6 us
    all_gather x1, blocking collectives, on_device(): rows_full = lax.all_gather(hidden, 'vocab', axis=1, tiled=True)  29.9 us
    all_to_all x1, waiting for transfers between devices, on_device(): lax.all_to_all(rows_full, 'dp', split_axis=1, concat_axis=0, tiled=True)  21.5 us
  transfers between devices with their start and end apart: 4, of which 4 were waited for; matrix products, arithmetic and copies ran while one was open for 3% of the time, Pallas kernels for 0%

commit v1 on v0

--- a/solution.py
+++ b/solution.py
@@ -73,7 +73,10 @@
     hidden_grad = lax.psum_scatter(
         hidden_term.astype(jnp.bfloat16), "vocab", scatter_dimension=1, tiled=True
     )
-    grad_cols = lax.all_to_all(rows_full, "dp", split_axis=1, concat_axis=0, tiled=True)
+    grad_cols = jnp.concatenate(
+        lax.all_to_all(jnp.stack(jnp.split(rows_full, lax.axis_size("dp"), axis=1)), "dp", 0, 0),
+        axis=0,
+    )
     head_grad = lax.dot_general(
         grad_cols,
         lax.all_gather(logit_grad, "dp", axis=0, tiled=True),

time: 487 us -> 493 us (1.012)
  waiting for transfers between devices: 260 us -> 244 us
  blocking collectives: 175 us -> 187 us
  local copies, waits for them, and re-layouts: 3.14 us -> 13.2 us
    all_to_all x1, waiting for transfers between devices: 21.5 us -> 0.01 us  [on_device(): lax.all_to_all(jnp.stack(jnp.split(rows_full, lax.axis_size('dp'), axis=1...]
    psum x1, blocking collectives: 32.6 us -> 46 us  [on_device(): summed_objective = lax.psum(group_objective, 'dp')]
    unnamed x7 -> x37, local copies, waits for them, and re-layouts: 1.32 us -> 11 us
    all_gather x1, waiting for transfers between devices: 48.8 us -> 57.2 us  [on_device(): lax.all_gather(logit_grad, 'dp', axis=0, tiled=True)]
  transfers between devices with their start and end apart: 4 -> 4, of which waited for: 4 -> 3; matrix products, arithmetic and copies ran while one was open for 3% -> 5% of each run, Pallas kernels for 0% -> 0%
where the time goes in v1:
time: 493 us; the launch traced here: 492 us
  waiting for transfers between devices  244 us (49%)
  blocking collectives  187 us (38%)
  matrix products  17.1 us (3%)
  between operations  16.9 us (3%)
  local copies, waits for them, and re-layouts  13.2 us (3%)
  starting transfers between devices  8.99 us (2%)
  other arithmetic  5.18 us (1%)
    reduce_scatter x1, waiting for transfers between devices, on_device(): lax.psum_scatter(hidden_term.astype(jnp.bfloat16), 'vocab', scatter_dimen...  104 us
    all_gather x1, waiting for transfers between devices, on_device(): weight_full = lax.all_gather(head_weight, 'dp', axis=0, tiled=True)  82.1 us
    all_gather x1, waiting for transfers between devices, on_device(): lax.all_gather(logit_grad, 'dp', axis=0, tiled=True)  57.2 us
    psum x1, blocking collectives, on_device(): lax.psum((jnp.sum(exp_student, axis=1), jnp.sum(exp_teacher, axis=1), jnp...  56.8 us
    pmax x1, blocking collectives, on_device(): max_student, max_teacher = lax.pmax((local_max, local_tmax), 'vocab')  56.2 us
    psum x1, blocking collectives, on_device(): summed_objective = lax.psum(group_objective, 'dp')  46 us
    all_gather x1, blocking collectives, on_device(): rows_full = lax.all_gather(hidden, 'vocab', axis=1, tiled=True)  27.6 us
    unnamed x37, local copies, waits for them, and re-layouts  11 us
  transfers between devices with their start and end apart: 4, of which 3 were waited for; matrix products, arithmetic and copies ran while one was open for 5% of the time, Pallas kernels for 0%

profile of v1, /device:TPU:2, one launch (start us, length us, event | category | flops | bytes accessed | tf_op | source)
XLA Modules:
  0.0 492.2 jit_solution(2252001102127599739)
XLA Ops:
  7.2 0.7 all-gather.3.cloned.1.call-update
  8.0 0.8 slice.7
  8.8 0.7 slice.6
  9.5 1.2 reduce_max.24
  10.7 27.6 %all_gather.9 = bf16[128,2048]{0,1:T(8,128)(2,1)S(1)} all-gather(bf16[128,64]{0,1:T(8,128)(2,1)} %param.6), channel_id=1, replica_groups=mesh['vocab'=32,'dp'=16] {'vocab'}, dimensions={1}, use_global_device_ids=true | all-gather | bytes 540672 | tf_op jit(solution)/shard_map/all_gather | solution.py:30
  38.4 82.1 %all-gather.3.cloned.1.call-done = bf16[2048,2048]{1,0:T(8,128)(2,1)} async-done(((bf16[128,2048]{1,0:T(8,128)(2,1)}), bf16[2048,2048]{1,0:T(8,128)(2,1)}) %all-gather.3.cloned.1.call-update) | async-done | bytes 8388624 | tf_op jit(solution)/shard_map/all_gather | solution.py:31
  120.5 4.7 fusion.15
  125.2 56.2 %all-reduce.1 = (f32[128]{0:T(128)S(1)}, f32[128]{0:T(128)S(1)}) all-reduce(bf16[128]{0:T(256)(128)(2,1)S(1)} %reduce_max.24, f32[128]{0:T(128)S(1)} %get-tuple-element.37), channel_id=1, replica_groups=mesh['vocab'=32,'dp'=16] {'vocab'}, use_global_device_ids=true, to_apply=%region_5.6 | all-reduce | flops 256 | bytes 1792 | tf_op jit(solution)/shard_map/pmax | solution.py:42
  181.4 0.8 fusion.6
  182.2 56.8 %all-reduce = (f32[128]{0:T(128)S(1)}, f32[128]{0:T(128)S(1)}, f32[128]{0:T(128)S(1)}, f32[128]{0:T(128)S(1)}, f32[128]{0:T(128)S(1)}) all-reduce(f32[128]{0:T(128)S(1)} %get-tuple-element.6, f32[128]{0:T(128)S(1)} %get-tuple-element.4, f32[128]{0:T(128)S(1)} %get-tuple-element.7, ...), channel_id=1, replica_groups=mesh['vocab'=32,'dp'=16] {'vocab'}, use_global_device_ids=true, to_apply=%region_11.12 | all-reduce | flops 640 | bytes 5120 | tf_op jit(solution)/shard_map/psum | solution.py:45
  239.0 0.6 add_reduce_fusion
  240.0 0.6 fusion.13
  240.8 1.4 fusion.11
  244.3 0.6 constant_dynamic-update-slice_fusion.15
  244.9 0.6 constant_dynamic-update-slice_fusion.14
  245.5 0.6 constant_dynamic-update-slice_fusion.13
  246.1 0.6 constant_dynamic-update-slice_fusion.12
  246.7 0.6 constant_dynamic-update-slice_fusion.11
  247.3 0.6 constant_dynamic-update-slice_fusion.10
  247.9 0.6 constant_dynamic-update-slice_fusion.9
  248.5 0.6 constant_dynamic-update-slice_fusion.8
  250.3 0.6 constant_dynamic-update-slice_fusion.5
  250.9 0.6 constant_dynamic-update-slice_fusion.4
  252.2 0.6 constant_dynamic-update-slice_fusion.2
  252.8 0.6 constant_dynamic-update-slice_fusion.1
  253.4 0.6 constant_dynamic-update-slice_fusion
  254.0 8.9 %all-to-all-start = ((bf16[16,128,128]{2,1,0:T(8,128)(2,1)}), bf16[16,128,128]{2,1,0:T(8,128)(2,1)S(1)}, u32[]{:S(2)}, u32[]{:S(2)}) async-start(bf16[16,128,128]{2,1,0:T(8,128)(2,1)} %constant_dynamic-update-slice_fusion), calls=%async_computation.1 | async-start | bytes 1048576 | tf_op jit(solution)/shard_map/all_to_all | solution.py:77
  262.9 6.7 %convolution_convert_fusion = bf16[128,2048]{0,1:T(8,128)(2,1)} fusion(bf16[128,2048]{1,0:T(8,128)(2,1)} %fusion.11, bf16[2048,2048]{1,0:T(8,128)(2,1)} %all-gather.3.cloned.1.call-done), kind=kOutput, calls=%fused_computation | convolution fusion | flops 1074003968 | bytes 9437184 | tf_op jit(solution)/shard_map/dot_general | solution.py:70
  270.9 46.0 %psum.47 = f32[]{:T(128)} all-reduce(f32[]{:T(128)S(6)} %add.55), channel_id=1, replica_groups=mesh['vocab'=32,'dp'=16] {'dp'}, use_global_device_ids=true, to_apply=%region_22.23 | all-reduce | flops 1 | bytes 8 | tf_op jit(solution)/shard_map/psum | solution.py:61
  317.5 57.2 %all-gather.5.cloned.1.call-done = bf16[2048,2048]{1,0:T(8,128)(2,1)} async-done(((bf16[128,2048]{1,0:T(8,128)(2,1)}), bf16[2048,2048]{1,0:T(8,128)(2,1)}) %all-gather.5.cloned.1.call-update) | async-done | bytes 8388624 | tf_op jit(solution)/shard_map/all_gather | solution.py:82
  374.7 5.6 %fusion.16 = f32[128,2048]{1,0:T(8,128)} fusion(bf16[2048,128]{1,0:T(8,128)(2,1)S(1)} %bitcast.41, bf16[2048,2048]{1,0:T(8,128)(2,1)} %all-gather.5.cloned.1.call-done), kind=kOutput, calls=%fused_computation.55 | convolution fusion | flops 1073741824 | bytes 9961472 | tf_op jit(solution)/shard_map/dot_general | solution.py:80
  380.4 104.2 %reduce-scatter.2.cloned.1.call-done = bf16[128,64]{0,1:T(8,128)(2,1)} async-done(((bf16[128,2048]{0,1:T(8,128)(2,1)}), bf16[128,64]{0,1:T(8,128)(2,1)}) %reduce-scatter.2.cloned.1.call-update) | async-done | bytes 16400 | tf_op jit(solution)/shard_map/reduce_scatter | solution.py:73
  (37 shorter events, 4.4 us)
Async XLA Ops:
  7.2 113.3 %all-gather.3.cloned.1.call-start = ((), (), s32[]{:S(2)}) async-start(), calls=%async_computation.2 | async-start | bytes 8912896 | tf_op jit(solution)/shard_map/all_gather | solution.py:31
  7.9 173.5 %copy-start = (bf16[128,2048]{1,0:T(8,128)(2,1)S(1)}, bf16[128,2048]{1,0:T(8,128)(2,1)}, u32[]{:S(2)}) copy-start(bf16[128,2048]{1,0:T(8,128)(2,1)} %param.8) | copy-start | bytes 1572868
  7.9 173.5 %copy-start.1 = (s32[128]{0:T(128)S(1)}, s32[128]{0:T(128)}, u32[]{:S(2)}) copy-start(s32[128]{0:T(128)} %param.9) | copy-start | bytes 1540
  7.9 366.8 %all-gather.5.cloned.1.call-start = ((), (), s32[]{:S(2)}) async-start(), calls=%async_computation.4 | async-start | bytes 8912896 | tf_op jit(solution)/shard_map/all_gather | solution.py:82
  38.4 201.3 %copy-start.2 = (s32[1,128]{1,0:T(1,128)S(1)}, s32[1,128]{1,0:T(1,128)}, u32[]{:S(2)}) copy-start(s32[1,128]{1,0:T(1,128)} %param.10) | copy-start | bytes 1540
  254.0 63.6 %all-to-all-start = ((bf16[16,128,128]{2,1,0:T(8,128)(2,1)}), bf16[16,128,128]{2,1,0:T(8,128)(2,1)S(1)}, u32[]{:S(2)}, u32[]{:S(2)}) async-start(bf16[16,128,128]{2,1,0:T(8,128)(2,1)} %constant_dynamic-update-slice_fusion), calls=%async_computation.1 | async-start | bytes 1048576 | tf_op jit(solution)/shard_map/all_to_all | solution.py:77
  262.9 221.7 %reduce-scatter.2.cloned.1.call-start = ((), (), s32[]{:S(2)}) async-start(), calls=%async_computation.3 | async-start | bytes 540672 | tf_op jit(solution)/shard_map/reduce_scatter | solution.py:73
Sparse Core Ops, SparseCore 0:
  10.1 110.3 all-gather.2
  242.4 132.3 all-gather.4
  379.6 104.8 reduce-scatter.1
